TPU v7x, 256 devices: a whole 4x4x8 slice. The times are simulated.
256 devices in a mesh: sample: 32 (over x, z_hi, core), tensor: 8 (over y, z_lo).
Axes of the slice: x: 4, y: 4, z: 8 (z_hi: 4, z_lo: 2; z = z_hi * 2 + z_lo), core: 2. Of those that a mesh axis runs over, the one named last changes fastest.
Arguments:
- prompt_x: bfloat16 [3072, 5120], P('sample'), may hold values from -6 to 6
- resp_x: bfloat16 [32, 256, 5120], P('sample'), may hold values from -6 to 6
- queries: bfloat16 [32, 256, 8192], P('sample', None, 'tensor'), may hold values from -8 to 8
- d_attn: bfloat16 [32, 256, 8192], P('sample', None, 'tensor'), may hold values from -6 to 6
- w_key: bfloat16 [5120, 1024], P(None, 'tensor'), may hold values from -0.078125 to 0.078125
- w_value: bfloat16 [5120, 1024], P(None, 'tensor'), may hold values from -0.078125 to 0.078125
- lengths: int32 [32], P('sample'), may hold values from 64 to 256, as said below
Outputs:
- d_queries: bfloat16 [32, 256, 8192], P('sample', None, 'tensor')
- d_resp_x: bfloat16 [32, 256, 5120], P('sample', None, 'tensor')
- d_prompt_x: bfloat16 [3072, 5120], P('sample', 'tensor')
- d_w_key: bfloat16 [5120, 1024], P('sample', 'tensor')
- d_w_value: bfloat16 [5120, 1024], P('sample', 'tensor')
Inputs may be any that keep to these rules, and one draw needn't show every extreme that they name: `lengths`: some response has all 256 tokens valid.
All inputs are finite; a program needn't handle non-finite values.
Results may differ from a plain program's by a relative error of at most 0.015.
The roundings to bfloat16 on the way count: a program that leaves them out, or rounds other values in their place, can miss the bound.
Values may be sent and summed in bfloat16 or wider, within the bound.
A program may use at most 128 MiB of HBM per device.

v0:
```python
import jax
import jax.numpy as jnp
from jax import lax
from jax.sharding import PartitionSpec as P

HD = 128


def rows_product(left, right):
    return lax.dot_general(
        left, right, (((0,), (0,)), ((), ())), preferred_element_type=jnp.float32
    )


def right_transposed(left, right):
    return lax.dot_general(
        left, right, (((1,), (1,)), ((), ())), preferred_element_type=jnp.float32
    )


def local(prompt_x, resp_x, queries, d_attn, w_key, w_value, lengths):
    scale = HD ** (-0.5)
    kv_width = w_key.shape[1]
    kv_heads = kv_width // HD
    q_heads = queries.shape[2] // HD
    pairs = q_heads // kv_heads // 2
    rlen = resp_x.shape[1]
    n_prompt = prompt_x.shape[0] * lax.axis_size("sample")
    total_keys = n_prompt + rlen
    hidden = resp_x[0]
    own_pk = jnp.dot(prompt_x, w_key, preferred_element_type=jnp.float32).astype(jnp.bfloat16)
    own_pv = jnp.dot(prompt_x, w_value, preferred_element_type=jnp.float32).astype(jnp.bfloat16)
    prompt_k, prompt_v = (
        lax.all_gather(own_pk, "sample", axis=0, tiled=True),
        lax.all_gather(own_pv, "sample", axis=0, tiled=True),
    )
    resp_k = jnp.dot(hidden, w_key, preferred_element_type=jnp.float32).astype(jnp.bfloat16)
    resp_v = jnp.dot(hidden, w_value, preferred_element_type=jnp.float32).astype(jnp.bfloat16)
    keys = jnp.concatenate([prompt_k, resp_k], 0).reshape(total_keys, kv_heads, HD)
    values = jnp.concatenate([prompt_v, resp_v], 0).reshape(total_keys, kv_heads, HD)
    valid = jnp.arange(rlen) < lengths[0]
    grad_in = jnp.where(valid[:, None], d_attn[0], jnp.zeros_like(d_attn[0]))
    query_blocks = jnp.moveaxis(queries[0].reshape(rlen, kv_heads, pairs, 2, HD), 2, 0)
    grad_blocks = jnp.moveaxis(grad_in.reshape(rlen, kv_heads, pairs, 2, HD), 2, 0)
    row_ids = jnp.arange(rlen)[:, None]
    col_ids = jnp.arange(total_keys)[None, :]
    allowed = (col_ids < n_prompt) | (col_ids - n_prompt <= row_ids)

    def head_block(carry, block):
        query, gout = block
        scores = (
            jnp.einsum("ikgd,jkd->kgij", query, keys, preferred_element_type=jnp.float32) * scale
        )
        scores = jnp.where(allowed, scores, -jnp.inf)
        top = jnp.max(scores, axis=-1, keepdims=True)
        expo = jnp.exp(scores - top)
        probs = expo / jnp.sum(expo, axis=-1, keepdims=True)
        probs_low = probs.astype(jnp.bfloat16)
        out = jnp.einsum("kgij,jkd->ikgd", probs_low, values, preferred_element_type=jnp.float32)
        row_dot = jnp.einsum("ikgd,ikgd->kgi", gout.astype(jnp.float32), out)
        grad_probs = jnp.einsum("ikgd,jkd->kgij", gout, values, preferred_element_type=jnp.float32)
        grad_scores = (probs * (grad_probs - row_dot[..., None])).astype(jnp.bfloat16)
        dq = (
            jnp.einsum("kgij,jkd->ikgd", grad_scores, keys, preferred_element_type=jnp.float32)
            * scale
        ).astype(jnp.bfloat16)
        acc_k = carry[0] + jnp.einsum(
            "kgij,ikgd->jkd", grad_scores, query, preferred_element_type=jnp.float32
        )
        acc_v = carry[1] + jnp.einsum(
            "kgij,ikgd->jkd", probs_low, gout, preferred_element_type=jnp.float32
        )
        return ((acc_k, acc_v), dq)

    zeros = jnp.zeros((total_keys, kv_heads, HD), jnp.float32)
    (acc_k, acc_v), dq_blocks = lax.scan(head_block, (zeros, zeros), (query_blocks, grad_blocks))
    d_queries = jnp.moveaxis(dq_blocks, 0, 2).reshape(1, rlen, q_heads * HD)
    grad_keys = acc_k.reshape(total_keys, kv_width) * scale
    grad_values = acc_v.reshape(total_keys, kv_width)
    sum_pk, sum_pv = (
        lax.psum_scatter(grad_keys[:n_prompt], "sample", scatter_dimension=0, tiled=True),
        lax.psum_scatter(grad_values[:n_prompt], "sample", scatter_dimension=0, tiled=True),
    )
    prompt_gk = sum_pk.astype(jnp.bfloat16)
    prompt_gv = sum_pv.astype(jnp.bfloat16)
    resp_gk = grad_keys[n_prompt:].astype(jnp.bfloat16)
    resp_gv = grad_values[n_prompt:].astype(jnp.bfloat16)
    resp_part = right_transposed(resp_gk, w_key) + right_transposed(resp_gv, w_value)
    prompt_part = right_transposed(prompt_gk, w_key) + right_transposed(prompt_gv, w_value)
    resp_dx, prompt_dx = (
        lax.psum_scatter(resp_part, "tensor", scatter_dimension=1, tiled=True),
        lax.psum_scatter(prompt_part, "tensor", scatter_dimension=1, tiled=True),
    )
    resp_grads = jnp.concatenate([resp_gk, resp_gv], 1)
    prompt_grads = jnp.concatenate([prompt_gk, prompt_gv], 1)
    weight_total = lax.psum_scatter(
        rows_product(hidden, resp_grads) + rows_product(prompt_x, prompt_grads),
        "sample",
        scatter_dimension=0,
        tiled=True,
    )
    d_w_key = weight_total[:, :kv_width].astype(jnp.bfloat16)
    d_w_value = weight_total[:, kv_width:].astype(jnp.bfloat16)
    return (
        d_queries,
        resp_dx.astype(jnp.bfloat16)[None],
        prompt_dx.astype(jnp.bfloat16),
        d_w_key,
        d_w_value,
    )


def solution(mesh):
    placed = (
        P("sample", None),
        P("sample", None, None),
        P("sample", None, "tensor"),
        P("sample", None, "tensor"),
        P(None, "tensor"),
        P(None, "tensor"),
        P("sample"),
    )
    return jax.shard_map(
        local,
        mesh=mesh,
        in_specs=placed,
        out_specs=(
            P("sample", None, "tensor"),
            P("sample", None, "tensor"),
            P("sample", "tensor"),
            P("sample", "tensor"),
            P("sample", "tensor"),
        ),
        check_vma=False,
    )
```

profile of v0, /device:TPU:1, one launch (start us, length us, event | category | flops | bytes accessed | tf_op | source)
XLA Modules:
  0.0 712.4 jit_solution(16998286236569792797)
XLA Ops:
  7.2 2.2 convolution_convert_fusion.1
  13.5 53.6 %all_gather.6 = bf16[3072,128]{1,0:T(8,128)(2,1)} all-gather(bf16[96,128]{1,0:T(8,128)(2,1)S(1)} %convolution_convert_fusion.1), channel_id=1, replica_groups=mesh['sample'=32,'tensor'=8] {'sample'}, dimensions={0}, use_global_device_ids=true | all-gather | bytes 811008 | tf_op jit(solution)/shard_map/all_gather | solution.py:34
  67.0 44.9 %all_gather.7 = bf16[3072,128]{1,0:T(8,128)(2,1)} all-gather(bf16[96,128]{1,0:T(8,128)(2,1)S(1)} %convolution_convert_fusion), channel_id=1, replica_groups=mesh['sample'=32,'tensor'=8] {'sample'}, dimensions={0}, use_global_device_ids=true | all-gather | bytes 811008 | tf_op jit(solution)/shard_map/all_gather | solution.py:35
  114.1 2.1 copy.28
  119.4 123.8 %while.15 = (s32[]{:T(128)}, f32[3328,1,128]{0,2,1:T(8,128)}, f32[3328,1,128]{0,2,1:T(8,128)}, bf16[4,256,1,2,128]{4,1,3,2,0:T(8,128)(2,1)}, bf16[4,256,1,2,128]...) while((s32[]{:T(128)}, f32[3328,1,128]{0,2,1:T(8,128)}, ...), condition=%wide.region_3.4_spmd.clone, body=%wide.region_0.3_spmd.clone.sunk | while | flops 2643130880 | bytes 119967792 | solution.py:76
  120.6 2.6 fusion.109
  124.3 1.8 copy-done.1
  126.1 2.7 fusion.111
  132.0 3.4 fusion.112
  135.5 5.5 fusion.113
  141.0 4.0 fusion.114
  147.0 1.9 fusion.115
  150.1 2.6 fusion.109
  153.8 1.8 copy-done.1
  155.6 2.7 fusion.111
  161.5 3.4 fusion.112
  165.0 5.5 fusion.113
  170.5 4.5 fusion.114
  177.0 3.3 fusion.115
  181.6 2.6 fusion.109
  185.2 1.8 copy-done.1
  187.0 2.7 fusion.111
  192.9 3.4 fusion.112
  196.4 5.5 fusion.113
  201.9 4.5 fusion.114
  208.4 3.3 fusion.115
  213.0 2.6 fusion.109
  216.7 1.8 copy-done.1
  218.4 2.7 fusion.111
  224.4 3.4 fusion.112
  227.8 5.5 fusion.113
  233.4 4.5 fusion.114
  239.9 3.3 fusion.115
  247.3 3.0 copy.44
  250.4 2.7 slice_bitcast_fusion.1
  253.1 3.1 copy.46
  256.3 77.8 %reduce-scatter.16.cloned.1.call-done = f32[96,128]{1,0:T(8,128)} async-done(((f32[3072,128]{1,0:T(8,128)}), f32[96,128]{1,0:T(8,128)}) %reduce-scatter.16.cloned.1.call-update) | async-done | bytes 49168
  335.0 3.2 fusion.61
  338.2 87.5 %reduce-scatter.18.cloned.1.call-done = f32[96,128]{1,0:T(8,128)} async-done(((f32[3072,128]{1,0:T(8,128)}), f32[96,128]{1,0:T(8,128)}) %reduce-scatter.18.cloned.1.call-update) | async-done | bytes 49168
  426.6 3.8 convolution_add_fusion.2
  432.9 3.2 fusion.35
  436.1 5.9 copy.48
  442.1 2.3 fusion.60
  444.4 3.2 convolution_add_fusion.1
  450.4 32.3 %reduce-scatter.14.cloned.1.call-done = f32[96,640]{1,0:T(8,128)} async-done(((f32[96,5120]{1,0:T(8,128)}), f32[96,640]{1,0:T(8,128)}) %reduce-scatter.14.cloned.1.call-update) | async-done | bytes 245776 | tf_op jit(solution)/shard_map/reduce_scatter | solution.py:92
  484.3 105.5 %reduce-scatter.20.cloned.1.call-done = f32[160,256]{1,0:T(8,128)} async-done(((f32[5120,256]{1,0:T(8,128)}), f32[160,256]{1,0:T(8,128)}) %reduce-scatter.20.cloned.1.call-update) | async-done | bytes 163856
  592.3 111.7 %reduce-scatter.12.cloned.1.call-done = f32[256,640]{1,0:T(8,128)} async-done(((f32[256,5120]{1,0:T(8,128)}), f32[256,640]{1,0:T(8,128)}) %reduce-scatter.12.cloned.1.call-update) | async-done | bytes 655376 | tf_op jit(solution)/shard_map/reduce_scatter | solution.py:91
  704.0 1.8 convert_bitcast_fusion
  (122 shorter events, 54.2 us)
Async XLA Ops:
  7.2 2.4 copy-start
  7.2 326.9 %reduce-scatter.16.cloned.1.call-start = ((), (), s32[]{:S(2)}) async-start(), calls=%async_computation.7 | async-start | bytes 1622016
  7.2 2.7 copy-start.6
  10.0 1.5 copy-start.7
  10.0 1.6 copy-start.9
  12.0 99.9 %copy-start.15 = (bf16[1,256,1024]{2,1,0:T(8,128)(2,1)S(1)}, bf16[1,256,1024]{2,1,0:T(8,128)(2,1)}, u32[]{:S(2)}) copy-start(bf16[1,256,1024]{2,1,0:T(8,128)(2,1)} %param.12) | copy-start | bytes 1572868
  116.2 1.4 copy-start.12
  116.2 2.4 copy-start.13
  116.2 2.4 copy-start.16
  123.2 2.8 copy-start.1
  132.0 3.4 copy-start.4
  132.0 3.4 copy-start.14
  141.0 4.0 copy-start.3
  145.0 2.0 copy-start.2
  145.0 2.0 copy-start.5
  152.7 2.8 copy-start.1
  161.5 3.4 copy-start.4
  161.5 3.4 copy-start.14
  170.5 4.5 copy-start.3
  175.0 2.0 copy-start.2
  175.0 2.0 copy-start.5
  184.2 2.8 copy-start.1
  192.9 3.4 copy-start.4
  192.9 3.4 copy-start.14
  201.9 4.5 copy-start.3
  206.5 2.0 copy-start.2
  206.5 2.0 copy-start.5
  215.6 2.8 copy-start.1
  224.4 3.4 copy-start.4
  224.4 3.4 copy-start.14
  233.4 4.5 copy-start.3
  237.9 2.0 copy-start.2
  237.9 2.0 copy-start.5
  244.8 1.2 copy-start.11
  250.4 175.4 %reduce-scatter.18.cloned.1.call-start = ((), (), s32[]{:S(2)}) async-start(), calls=%async_computation.8 | async-start | bytes 1622016
  256.2 226.4 %reduce-scatter.14.cloned.1.call-start = ((), (), s32[]{:S(2)}) async-start(), calls=%async_computation.6 | async-start | bytes 2211840 | tf_op jit(solution)/shard_map/reduce_scatter | solution.py:92
  430.4 159.4 %reduce-scatter.20.cloned.1.call-start = ((), (), s32[]{:S(2)}) async-start(), calls=%async_computation.9 | async-start | bytes 5406720
  431.7 1.2 copy-start.10
  442.0 262.0 %reduce-scatter.12.cloned.1.call-start = ((), (), s32[]{:S(2)}) async-start(), calls=%async_computation.5 | async-start | bytes 5898240 | tf_op jit(solution)/shard_map/reduce_scatter | solution.py:91
  442.1 2.3 copy-start.8
Sparse Core Ops, SparseCore 0:
  250.5 83.5 reduce-scatter.15
  337.9 87.7 reduce-scatter.17
  430.6 52.0 reduce-scatter.13
  487.1 102.6 reduce-scatter.19
  592.2 111.7 reduce-scatter.11
where the time goes:
time: 714 us; the launch traced here: 712 us
  waiting for transfers between devices  415 us (58%)
  matrix products  104 us (15%)
  blocking collectives  98.4 us (14%)
  local copies, waits for them, and re-layouts  50.5 us (7%)
  other arithmetic  29.5 us (4%)
  between operations  14.6 us (2%)
    unnamed x8, waiting for transfers between devices  271 us
    reduce_scatter x1, waiting for transfers between devices, local(): lax.psum_scatter(resp_part, 'tensor', scatter_dimension=1, tiled=True)  112 us
    all_gather x1, blocking collectives, local(): lax.all_gather(own_pk, 'sample', axis=0, tiled=True)  53.6 us
    all_gather x1, blocking collectives, local(): lax.all_gather(own_pv, 'sample', axis=0, tiled=True)  44.9 us
    reduce_scatter x1, waiting for transfers between devices, local(): lax.psum_scatter(prompt_part, 'tensor', scatter_dimension=1, tiled=True)  32.3 us
    dot_general x4, matrix products, head_block(): jnp.einsum('ikgd,jkd->kgij', gout, values, preferred_element_type=jnp.flo...  22.2 us
    unnamed x32, local copies, waits for them, and re-layouts  21.7 us
    dot_general x4, matrix products, head_block(): jnp.einsum('kgij,ikgd->jkd', grad_scores, query, preferred_element_type=j...  17.5 us
  transfers between devices with their start and end apart: 5, of which 5 were waited for; matrix products, arithmetic and copies ran while one was open for 5% of the time, Pallas kernels for 0%

commit v1 on v0

v1 whole, which is shorter than its diff:
```python
import functools
import math

import jax
import jax.numpy as jnp
from jax import lax
from jax.experimental import pallas as pl
from jax.experimental.pallas import tpu as pltpu
from jax.sharding import PartitionSpec as P

f32 = jnp.float32
bf16 = jnp.bfloat16
MESH = pl.DeviceIdType.MESH
HD = 128
HEADS = 8
RL = 256
NX, NZ, NC, NY, NL = 4, 4, 2, 4, 2
NT = NY * NL
PR = 96
BLK = NZ * NC * PR
NP = NX * BLK
DM = 5120
DR = DM // (NX * NZ * NC)
DT = DM // NT
SCALE = HD**-0.5
SCALE2 = SCALE * math.log2(math.e)


def dot(a, b):
    return lax.dot_general(a, b, (((1,), (0,)), ((), ())), preferred_element_type=f32)


def dot_t(a, b):
    return lax.dot_general(a, b, (((1,), (1,)), ((), ())), preferred_element_type=f32)


def offset(k):
    return k + k // 2 - 2 * (k // 3)


def kernel(
    px_hbm, rx_hbm, q_hbm, g_hbm, wk_hbm, wv_hbm, len_ref,
    dq_hbm, drx_hbm, dpx_hbm, dwk_hbm, dwv_hbm,
    px, rx, q_in, g_in, w, rxt, pxt,
    kv, kvt, qa, ga, qt, gt,
    e_ref, er_ref, gs_ref, s_ref, mc_ref, m_ref, mm, ll, oo, al_ref, be_ref, rd, dqt,
    gblk, keep, rcs, rcr, rxs, rxr, rzs, rzr, zacc,
    rg_all, pg_all, wsl, dwr, dkeep, dcs, dcr, dxs, dxr, dzs, dzr,
    dq_out, drx_out, dpx_out, dw_out,
    ld_sem, out_sem,
    agz_s, agz_r, agx_s, agx_r, agc_s, agc_r,
    w_s, w_r, wc_s, wc_r, t_s, t_r,
    rc_s, rc_r, rx_s, rx_r, rz_s, rz_r, p_s, p_r,
    dc_s, dc_r, dx_s, dx_r, dz_s, dz_r,
):
    sm = lax.axis_index("sample")
    tn = lax.axis_index("tensor")
    c = lax.rem(sm, NC)
    z = lax.rem(sm // NC, NZ)
    x = sm // (NC * NZ)
    y = tn // NL
    lo = lax.rem(tn, NL)
    oc = 1 - c

    def dev_s(xx, zz, cc):
        return ((xx * NZ + zz) * NC + cc, tn)

    core = dev_s(x, z, oc)

    def dev_x(o):
        return dev_s(lax.rem(x + o, NX), z, c)

    def dev_z(o):
        return dev_s(x, lax.rem(z + o, NZ), c)

    def dev_t(o):
        return (sm, lax.rem(tn + o, NT))

    def dev_y(o):
        return (sm, lax.rem(y + o, NY) * NL + lo)

    dev_l = (sm, y * NL + 1 - lo)

    def remote(src, dst, ss, rs, dev):
        return pltpu.make_async_remote_copy(
            src_ref=src, dst_ref=dst, send_sem=ss, recv_sem=rs, device_id=dev,
            device_id_type=MESH,
        )

    def al(v, n):
        return pl.multiple_of(v, n)

    loads = [
        pltpu.make_async_copy(px_hbm, px, ld_sem.at[0]),
        pltpu.make_async_copy(wk_hbm, w.at[:, pl.ds(0, HD)], ld_sem.at[1]),
        pltpu.make_async_copy(wv_hbm, w.at[:, pl.ds(HD, HD)], ld_sem.at[2]),
        pltpu.make_async_copy(rx_hbm.at[0], rx, ld_sem.at[3]),
        pltpu.make_async_copy(q_hbm.at[0], q_in, ld_sem.at[4]),
        pltpu.make_async_copy(g_hbm.at[0], g_in, ld_sem.at[5]),
    ]
    for cp in loads:
        cp.start()

    barrier = pltpu.get_barrier_semaphore()
    peers = [core] + [dev_x(o) for o in (1, 2, 3)] + [dev_z(o) for o in (1, 2, 3)]
    peers += [dev_t(o) for o in range(1, NT)]
    for dev in peers:
        pl.semaphore_signal(barrier, inc=1, device_id=dev, device_id_type=MESH)

    loads[0].wait()
    loads[1].wait()
    loads[2].wait()

    def chunk(xx, zz, cc):
        return pl.ds(al(((xx * NZ + zz) * NC + cc) * PR, PR), PR)

    kv[chunk(x, z, c), :] = dot(px[...], w[...]).astype(bf16)
    pl.semaphore_wait(barrier, len(peers))

    def ag_z(i):
        rows = chunk(x, z, c)
        return remote(kv.at[rows, :], kv.at[rows, :], agz_s.at[i], agz_r.at[i], dev_z(i + 1))

    def ag_x(j, i):
        rows = chunk(x, lax.rem(z - j + NZ, NZ), c)
        return remote(
            kv.at[rows, :], kv.at[rows, :], agx_s.at[i, j], agx_r.at[i, j],
            dev_x(offset(i + 1)),
        )

    def ag_c(k, j):
        rows = chunk(lax.rem(x - offset(k) + NX, NX), lax.rem(z - j + NZ, NZ), c)
        return remote(kv.at[rows, :], kv.at[rows, :], agc_s.at[k, j], agc_r.at[k, j], core)

    for i in range(3):
        ag_z(i).start()
    for i in range(3):
        ag_x(0, i).start()
    ag_c(0, 0).start()

    loads[3].wait()
    kv[NP : NP + RL, :] = dot(rx[...], w[...]).astype(bf16)
    loads[4].wait()
    loads[5].wait()
    valid = lax.broadcasted_iota(jnp.int32, (RL, HD), 0) < len_ref[0]
    for h in range(HEADS):
        qh = q_in[:, h * HD : (h + 1) * HD]
        gh = jnp.where(valid, g_in[:, h * HD : (h + 1) * HD], jnp.zeros((RL, HD), bf16))
        qa[h * RL : (h + 1) * RL, :] = qh
        ga[h * RL : (h + 1) * RL, :] = gh
        qt[h] = qh.T
        gt[h] = gh.T
    kvt[NX, :, 0:RL] = kv[NP : NP + RL, :].T

    for j in range(1, NZ):
        ag_z(j - 1).wait_recv()
        for i in range(3):
            ag_x(j, i).start()
        ag_c(0, j).start()

    def hc(h):
        return slice(h * RL, (h + 1) * RL)

    def scores(base, n, h, first):
        s = dot(kv[pl.ds(base, n), 0:HD], qt[h])
        if first:
            ri = lax.broadcasted_iota(jnp.int32, (RL, RL), 0)
            ci = lax.broadcasted_iota(jnp.int32, (RL, RL), 1)
            s = jnp.where(ri <= ci, s, -jnp.inf)
        s_ref[h % 2, 0:n, :] = s
        mc_ref[h % 2] = jnp.max(s, axis=0, keepdims=True) * SCALE2

    def expo(slot, n, h, first):
        mc = mc_ref[h % 2]
        e = jnp.exp2(s_ref[h % 2, 0:n, :] * SCALE2 - mc)
        lc = jnp.sum(e, axis=0, keepdims=True)
        if first:
            er_ref[:, hc(h)] = e.astype(bf16)
        else:
            e_ref[slot, :, hc(h)] = e.astype(bf16)
        m_ref[slot, h] = mc
        if first:
            mm[h] = mc
            ll[h] = lc
        else:
            mo = mm[h]
            mn = jnp.maximum(mo, mc)
            a = jnp.exp2(mo - mn)
            b = jnp.exp2(mc - mn)
            mm[h] = mn
            ll[h] = ll[h] * a + lc * b
            al_ref[h] = a
            be_ref[h] = b

    def outs(slot, n, h, first):
        e = er_ref[:, hc(h)] if first else e_ref[slot, :, hc(h)]
        o = dot(kvt[slot, HD : 2 * HD, 0:n], e)
        oo[h] = o if first else oo[h] * al_ref[h] + o * be_ref[h]

    def pass1(slot, base, n, first):
        scores(base, n, 0, first)
        for h in range(HEADS):
            if h < HEADS - 1:
                scores(base, n, h + 1, first)
            expo(slot, n, h, first)
            if h:
                outs(slot, n, h - 1, first)
        outs(slot, n, HEADS - 1, first)

    pass1(NX, NP, RL, True)

    def block_of(k):
        return al(lax.rem(x - offset(k) + NX, NX) * BLK, BLK)

    def blocks1(k, _):
        @pl.when(k < NX - 1)
        def _():
            for j in range(NZ):
                ag_x(j, k).wait_recv()
                ag_c(k + 1, j).start()

        for j in range(NZ):
            ag_c(k, j).wait_recv()
        base = block_of(k)
        kvt[k] = kv[pl.ds(base, BLK), :].T
        pass1(k, base, BLK, False)
        return 0

    lax.fori_loop(0, NX, blocks1, 0)

    def w_send(o):
        t2 = lax.rem(tn + o, NT)
        src = w.at[pl.ds(al(t2 * DT + c * (DT // 2), DT // 2), DT // 2), :]
        dst = wsl.at[tn, pl.ds(al(c * (DT // 2), DT // 2), DT // 2), :]
        return remote(src, dst, w_s.at[o - 1], w_r.at[o - 1], dev_t(o))

    def w_core(o):
        ref = wsl.at[
            lax.rem(tn - o + NT, NT), pl.ds(al(c * (DT // 2), DT // 2), DT // 2), :
        ]
        return remote(ref, ref, wc_s.at[o - 1], wc_r.at[o - 1], core)

    for o in range(1, NT):
        w_send(o).start()

    for h in range(HEADS):
        rl = 1.0 / ll[h]
        rd[h] = jnp.sum(gt[h].astype(f32) * (oo[h] * rl), axis=0, keepdims=True)
        ll[h] = rl
        dqt[h] = jnp.zeros((HD, RL), f32)

    def grads(base, n, h):
        s_ref[h % 2, 0:n, :] = dot(kv[pl.ds(base, n), HD : 2 * HD], gt[h])

    def gscores(slot, n, h, first):
        fac = jnp.exp2(m_ref[slot, h] - mm[h]) * ll[h]
        e = er_ref[:, hc(h)] if first else e_ref[slot, :, hc(h)]
        p = e.astype(f32) * fac
        pb = p.astype(bf16)
        if first:
            er_ref[:, hc(h)] = pb
        else:
            e_ref[slot, :, hc(h)] = pb
        gs_ref[0:n, hc(h)] = (p * (s_ref[h % 2, 0:n, :] - rd[h])).astype(bf16)

    def dqs(slot, n, h):
        dqt[h] += dot(kvt[slot, 0:HD, 0:n], gs_ref[0:n, hc(h)])

    def pass2(slot, base, n, first, heads=range(HEADS)):
        grads(base, n, heads[0])
        for h in heads:
            if h < heads[-1]:
                grads(base, n, h + 1)
            gscores(slot, n, h, first)
            if h > heads[0]:
                dqs(slot, n, h - 1)
        dqs(slot, n, heads[-1])

    def key_grads(slot, n, first):
        pb = er_ref[...] if first else e_ref[slot]
        gblk[0:n, 0:HD] = dot(gs_ref[0:n, :], qa[...]) * SCALE
        gblk[0:n, HD : 2 * HD] = dot(pb, ga[...])

    pass2(NX, NP, RL, True)
    key_grads(NX, RL, True)
    rg_all[tn] = gblk[0:RL, :].astype(bf16)

    def t_own(i):
        ref = rg_all.at[tn]
        return remote(ref, ref, t_s.at[i], t_r.at[i], dev_l if i == 0 else dev_y(i))

    def t_fwd(i):
        ref = rg_all.at[y * NL + 1 - lo]
        return remote(ref, ref, t_s.at[3 + i], t_r.at[3 + i], dev_y(i))

    for i in range(4):
        t_own(i).start()

    def rs_c(k):
        return remote(rcs.at[k], rcr.at[k], rc_s.at[k], rc_r.at[k], core)

    def rs_x(k):
        return remote(rxs.at[k], rxr.at[k], rx_s.at[k], rx_r.at[k], dev_x(NX - offset(NX - 1 - k)))

    def rs_z(i):
        return remote(rzs.at[i], rzr.at[i], rz_s.at[i], rz_r.at[i], dev_z(i + 1))

    def blocks2(k, _):
        slot = NX - 1 - k
        base = block_of(slot)
        pass2(slot, base, BLK, False, range(0, HEADS // 2))

        @pl.when(k > 0)
        def _():
            rs_c(k - 1).wait_recv()
            for zz in range(NZ):
                rxs[k - 1, zz] = (keep[k - 1, zz] + rcr[k - 1, zz].astype(f32)).astype(bf16)
            rs_x(k - 1).start()

        pass2(slot, base, BLK, False, range(HEADS // 2, HEADS))
        key_grads(slot, BLK, False)
        for zz in range(NZ):
            rcs[k, zz] = gblk[pl.ds(al((zz * NC + oc) * PR, PR), PR), :].astype(bf16)
            keep[k, zz] = gblk[pl.ds(al((zz * NC + c) * PR, PR), PR), :]
        rs_c(k).start()

        @pl.when(k == 1)
        def _():
            t_own(0).wait_recv()
            for i in range(1, 4):
                t_fwd(i).start()

        return 0

    lax.fori_loop(0, NX, blocks2, 0)

    for h in range(HEADS):
        dq_out[:, h * HD : (h + 1) * HD] = (dqt[h].T * SCALE).astype(bf16)
    out_dq = pltpu.make_async_copy(dq_out, dq_hbm.at[0], out_sem.at[0])
    out_dq.start()

    rs_c(NX - 1).wait_recv()
    for k in range(NX - 1):
        rs_x(k).wait_recv()
    for zz in range(NZ):
        tot = keep[NX - 1, zz] + rcr[NX - 1, zz].astype(f32)
        for k in range(NX - 1):
            tot = tot + rxr[k, zz].astype(f32)
        zacc[zz] = tot
    for i in range(3):
        rzs[i] = zacc[lax.rem(z + i + 1, NZ)].astype(bf16)
        rs_z(i).start()

    for o in range(1, NT):
        w_send(o).wait_recv()
        w_core(o).start()
    wsl[tn] = w[pl.ds(al(tn * DT, DT), DT), :]
    pxt[...] = px[...].T
    rxt[...] = rx[...].T
    own_rg = rg_all[tn]
    for i in range(NX):
        rows = slice(i * (DM // NX), (i + 1) * (DM // NX))
        dwr[rows, :] = dot(rxt[rows, :], own_rg)

    for i in range(3):
        rs_z(i).wait_recv()
    tot = zacc[z]
    for i in range(3):
        tot = tot + rzr[i].astype(f32)
    pg = tot.astype(bf16)
    pg_all[tn] = pg

    def p_send(o):
        return remote(pg_all.at[tn], pg_all.at[tn], p_s.at[o - 1], p_r.at[o - 1], dev_t(o))

    def dw_c(g):
        return remote(dcs.at[g], dcr.at[g], dc_s.at[g], dc_r.at[g], core)

    def dw_x(g, i):
        return remote(
            dxs.at[g, i], dxr.at[g, i], dx_s.at[g, i], dx_r.at[g, i], dev_x(offset(3 - i))
        )

    def dw_z(g):
        return remote(dzs.at[g], dzr.at[g], dz_s.at[g], dz_r.at[g], dev_z(offset(3 - g)))

    def dw_group(g, _):
        zz = lax.rem(z + offset(3 - g), NZ)
        for i in range(NX):
            xx = lax.rem(x + offset(3 - i), NX)
            first = (xx * NZ + zz) * NC
            theirs = pl.ds(al((first + oc) * DR, DR), DR)
            mine = pl.ds(al((first + c) * DR, DR), DR)
            dcs[g, i] = (dwr[theirs, :] + dot(pxt[theirs, :], pg)).astype(bf16)
            dkeep[g, i] = dwr[mine, :] + dot(pxt[mine, :], pg)
        dw_c(g).start()
        return 0

    lax.fori_loop(0, NZ, dw_group, 0)
    for o in range(1, NT):
        p_send(o).start()

    def dw_sum(g, _):
        dw_c(g).wait_recv()
        for i in range(NX - 1):
            dxs[g, i] = (dkeep[g, i] + dcr[g, i].astype(f32)).astype(bf16)
            dw_x(g, i).start()
        dkeep[g, NX - 1] = dkeep[g, NX - 1] + dcr[g, NX - 1].astype(f32)
        return 0

    lax.fori_loop(0, NZ, dw_sum, 0)

    for i in range(1, 4):
        t_own(i).wait_recv()
        t_fwd(i).wait_recv()
    for o in range(1, NT):
        w_core(o).wait_recv()
    acc = dot_t(rg_all[0], wsl[0])
    for t2 in range(1, NT):
        acc = acc + dot_t(rg_all[t2], wsl[t2])
    drx_out[...] = acc.astype(bf16)
    out_drx = pltpu.make_async_copy(drx_out, drx_hbm.at[0], out_sem.at[1])
    out_drx.start()

    def dw_last(g, _):
        for i in range(NX - 1):
            dw_x(g, i).wait_recv()
        tot = dkeep[g, NX - 1]
        for i in range(NX - 1):
            tot = tot + dxr[g, i].astype(f32)
        dkeep[g, NX - 1] = tot

        @pl.when(g < NZ - 1)
        def _():
            dzs[g] = tot.astype(bf16)
            dw_z(g).start()

        return 0

    lax.fori_loop(0, NZ, dw_last, 0)

    for o in range(1, NT):
        p_send(o).wait_recv()
    acc = dot_t(pg_all[0], wsl[0])
    for t2 in range(1, NT):
        acc = acc + dot_t(pg_all[t2], wsl[t2])
    dpx_out[...] = acc.astype(bf16)
    out_dpx = pltpu.make_async_copy(dpx_out, dpx_hbm, out_sem.at[2])
    out_dpx.start()

    for g in range(NZ - 1):
        dw_z(g).wait_recv()
    tot = dkeep[NZ - 1, NX - 1]
    for g in range(NZ - 1):
        tot = tot + dzr[g].astype(f32)
    dw_out[0] = tot[:, 0:HD].astype(bf16)
    dw_out[1] = tot[:, HD : 2 * HD].astype(bf16)
    out_dwk = pltpu.make_async_copy(dw_out.at[0], dwk_hbm, out_sem.at[3])
    out_dwv = pltpu.make_async_copy(dw_out.at[1], dwv_hbm, out_sem.at[4])
    out_dwk.start()
    out_dwv.start()

    for i in range(3):
        ag_z(i).wait_send()
        for j in range(NZ):
            ag_x(j, i).wait_send()
        rs_x(i).wait_send()
        rs_z(i).wait_send()
        dw_z(i).wait_send()
    for k in range(NX):
        for j in range(NZ):
            ag_c(k, j).wait_send()
        rs_c(k).wait_send()
        dw_c(k).wait_send()
        for i in range(NX - 1):
            dw_x(k, i).wait_send()
    for o in range(1, NT):
        w_send(o).wait_send()
        w_core(o).wait_send()
        p_send(o).wait_send()
    for i in range(4):
        t_own(i).wait_send()
    for i in range(1, 4):
        t_fwd(i).wait_send()
    for cp in (out_dq, out_drx, out_dpx, out_dwk, out_dwv):
        cp.wait()


def local(prompt_x, resp_x, queries, d_attn, w_key, w_value, lengths):
    any_ = pl.BlockSpec(memory_space=pl.ANY)
    v = pltpu.VMEM
    dma = pltpu.SemaphoreType.DMA
    scratch = [
        v((PR, DM), bf16), v((RL, DM), bf16), v((RL, HEADS * HD), bf16), v((RL, HEADS * HD), bf16),
        v((DM, 2 * HD), bf16), v((DM, RL), bf16), v((DM, PR), bf16),
        v((NP + RL, 2 * HD), bf16), v((NX + 1, 2 * HD, BLK), bf16),
        v((HEADS * RL, HD), bf16), v((HEADS * RL, HD), bf16),
        v((HEADS, HD, RL), bf16), v((HEADS, HD, RL), bf16),
        v((NX, BLK, HEADS * RL), bf16), v((RL, HEADS * RL), bf16), v((BLK, HEADS * RL), bf16),
        v((2, BLK, RL), f32), v((2, 1, RL), f32), v((NX + 1, HEADS, 1, RL), f32),
        v((HEADS, 1, RL), f32), v((HEADS, 1, RL), f32), v((HEADS, HD, RL), f32),
        v((HEADS, 1, RL), f32), v((HEADS, 1, RL), f32), v((HEADS, 1, RL), f32),
        v((HEADS, HD, RL), f32),
        v((BLK, 2 * HD), f32), v((NX, NZ, PR, 2 * HD), f32),
        v((NX, NZ, PR, 2 * HD), bf16), v((NX, NZ, PR, 2 * HD), bf16),
        v((3, NZ, PR, 2 * HD), bf16), v((3, NZ, PR, 2 * HD), bf16),
        v((3, PR, 2 * HD), bf16), v((3, PR, 2 * HD), bf16), v((NZ, PR, 2 * HD), f32),
        v((NT, RL, 2 * HD), bf16), v((NT, PR, 2 * HD), bf16), v((NT, DT, 2 * HD), bf16),
        v((DM, 2 * HD), f32), v((NZ, NX, DR, 2 * HD), f32),
        v((NZ, NX, DR, 2 * HD), bf16), v((NZ, NX, DR, 2 * HD), bf16),
        v((NZ, NX - 1, DR, 2 * HD), bf16), v((NZ, NX - 1, DR, 2 * HD), bf16),
        v((NZ - 1, DR, 2 * HD), bf16), v((NZ - 1, DR, 2 * HD), bf16),
        v((RL, HEADS * HD), bf16), v((RL, DT), bf16), v((PR, DT), bf16), v((2, DR, HD), bf16),
        dma((6,)), dma((5,)),
        dma((3,)), dma((3,)), dma((3, NZ)), dma((3, NZ)), dma((NX, NZ)), dma((NX, NZ)),
        dma((NT - 1,)), dma((NT - 1,)), dma((NT - 1,)), dma((NT - 1,)),
        dma((NT - 1,)), dma((NT - 1,)),
        dma((NX,)), dma((NX,)), dma((3,)), dma((3,)), dma((3,)), dma((3,)),
        dma((NT - 1,)), dma((NT - 1,)),
        dma((NZ,)), dma((NZ,)), dma((NZ, 3)), dma((NZ, 3)), dma((3,)), dma((3,)),
    ]
    return pl.pallas_call(
        kernel,
        out_shape=(
            jax.ShapeDtypeStruct((1, RL, HEADS * HD), bf16),
            jax.ShapeDtypeStruct((1, RL, DT), bf16),
            jax.ShapeDtypeStruct((PR, DT), bf16),
            jax.ShapeDtypeStruct((DR, HD), bf16),
            jax.ShapeDtypeStruct((DR, HD), bf16),
        ),
        in_specs=[any_] * 6 + [pl.BlockSpec(memory_space=pltpu.SMEM)],
        out_specs=(any_,) * 5,
        scratch_shapes=scratch,
        compiler_params=pltpu.CompilerParams(
            collective_id=0, has_side_effects=True, vmem_limit_bytes=63 * 2**20
        ),
        name="kv_backward",
    )(prompt_x, resp_x, queries, d_attn, w_key, w_value, lengths)


def solution(mesh):
    placed = (
        P("sample", None),
        P("sample", None, None),
        P("sample", None, "tensor"),
        P("sample", None, "tensor"),
        P(None, "tensor"),
        P(None, "tensor"),
        P("sample"),
    )
    return jax.shard_map(
        local,
        mesh=mesh,
        in_specs=placed,
        out_specs=(
            P("sample", None, "tensor"),
            P("sample", None, "tensor"),
            P("sample", "tensor"),
            P("sample", "tensor"),
            P("sample", "tensor"),
        ),
        check_vma=False,
    )
```

time: 714 us -> 100 us (0.14)
  waiting for transfers between devices: 415 us -> 0 us
  matrix products: 104 us -> 0 us
  blocking collectives: 98.4 us -> 0 us
  Pallas kernels: 0 us -> 93.3 us
  local copies, waits for them, and re-layouts: 50.5 us -> 5.53 us
  other arithmetic: 29.5 us -> 0 us
  between operations: 14.6 us -> 1.32 us
    unnamed x8 -> x0, waiting for transfers between devices: 271 us -> none
    reduce_scatter x2 -> x0, waiting for transfers between devices: 144 us -> none  [the longest x1 112 us: local(): lax.psum_scatter(resp_part, 'tensor', scatter_dimension=1, tiled=True)]
    dot_general x34 -> x0, matrix products: 104 us -> none  [the longest x4 22.2 us: head_block(): jnp.einsum('ikgd,jkd->kgij', gout, values, preferred_element_type=jnp.flo...]
    all_gather x2 -> x0, blocking collectives: 98.4 us -> none  [the longest x1 53.6 us: local(): lax.all_gather(own_pk, 'sample', axis=0, tiled=True)]
    pallas_call x0 -> x1, Pallas kernels: none -> 93.3 us  [local(): pl.pallas_call(kernel, out_shape=(jax.ShapeDtypeStruct((1, RL, HEADS * HD...]
    unnamed x32 -> x11, local copies, waits for them, and re-layouts: 21.7 us -> 5.53 us
    dynamic_slice x8 -> x0, local copies, waits for them, and re-layouts: 12.9 us -> none  [local(): lax.scan(head_block, (zeros, zeros), (query_blocks, grad_blocks))]
    convert_element_type x5 -> x0, other arithmetic: 12.5 us -> none  [the longest x4 10.9 us: head_block(): probs_low = probs.astype(jnp.bfloat16)]
  transfers between devices with their start and end apart: 5 -> 0, of which waited for: 5 -> 0; matrix products, arithmetic and copies ran while one was open for 5% -> 0% of each run, Pallas kernels for 0% -> 0%
where the time goes in v1:
time: 100 us
  Pallas kernels  93.3 us (93%)
  local copies, waits for them, and re-layouts  5.53 us (6%)
  between operations  1.32 us (1%)
    pallas_call x1, Pallas kernels, local(): pl.pallas_call(kernel, out_shape=(jax.ShapeDtypeStruct((1, RL, HEADS * HD...  93.3 us
    unnamed x11, local copies, waits for them, and re-layouts  5.53 us

profile of v1, /device:TPU:1, one launch (start us, length us, event | category | flops | bytes accessed | tf_op | source)
XLA Modules:
  0.0 100.1 jit_solution(12087097397883759584)
XLA Ops:
  1.3 93.3 %kv_backward.1 = (bf16[1,256,1024]{2,1,0:T(8,128)(2,1)}, bf16[1,256,640]{2,1,0:T(8,128)(2,1)}, bf16[96,640]{1,0:T(8,128)(2,1)}, bf16[160,128]{1,0:T(8,128)(2,1)}, bf16[160,128]{1,0:T(8,128)(2,1)}) custom-call(bf16[96,5120]{1,0:T(8,128)(2,1)} %px_hbm.1, bf16[1,256,5120]{2,1,0:T(8,128)(2,1)} %rx_hbm.1, bf16[1,256,1024]{2,1,0:T(8,128)(2,1)} %q_hbm.1, ...), custom_call_target="tpu_custom_call" | custom-call | tf_op jit(solution)/shard_map/kv_backward/pallas_call | solution.py:522
  94.6 0.0 copy-start
  94.6 0.0 copy-start.2
  94.6 0.0 copy-start.1
  94.6 1.9 %copy.18 = bf16[1,256,1024]{2,1,0:T(8,128)(2,1)} copy(bf16[1,256,1024]{2,1,0:T(8,128)(2,1)} %get-tuple-element.10) | data formatting | bytes 1048576
  96.5 1.7 %copy.19 = bf16[1,256,640]{2,1,0:T(8,128)(2,1)} copy(bf16[1,256,640]{2,1,0:T(8,128)(2,1)} %get-tuple-element.11) | data formatting | bytes 655360
  98.2 0.0 copy-done
  98.2 0.6 copy.20
  98.9 0.0 copy-done.2
  98.9 0.6 copy.21
  99.5 0.0 copy-done.1
  99.5 0.6 copy.22
Async XLA Ops:
  94.6 3.7 %copy-start = (bf16[96,640]{1,0:T(8,128)(2,1)S(1)}, bf16[96,640]{1,0:T(8,128)(2,1)}, u32[]{:S(2)}) copy-start(bf16[96,640]{1,0:T(8,128)(2,1)} %get-tuple-element.12) | copy-start | bytes 368644
  94.6 4.3 %copy-start.2 = (bf16[160,128]{1,0:T(8,128)(2,1)S(1)}, bf16[160,128]{1,0:T(8,128)(2,1)}, u32[]{:S(2)}) copy-start(bf16[160,128]{1,0:T(8,128)(2,1)} %get-tuple-element.13) | copy-start | bytes 122884
  94.6 4.9 %copy-start.1 = (bf16[160,128]{1,0:T(8,128)(2,1)S(1)}, bf16[160,128]{1,0:T(8,128)(2,1)}, u32[]{:S(2)}) copy-start(bf16[160,128]{1,0:T(8,128)(2,1)} %get-tuple-element.14) | copy-start | bytes 122884

commit v2 on v1

--- a/solution.py
+++ b/solution.py
@@ -17,8 +17,8 @@
 NX, NZ, NC, NY, NL = 4, 4, 2, 4, 2
 NT = NY * NL
 PR = 96
-BLK = NZ * NC * PR
-NP = NX * BLK
+BLK = NX * NC * PR
+NP = NZ * BLK
 DM = 5120
 DR = DM // (NX * NZ * NC)
 DT = DM // NT
@@ -44,7 +44,7 @@
     px, rx, q_in, g_in, w, rxt, pxt,
     kv, kvt, qa, ga, qt, gt,
     e_ref, er_ref, gs_ref, s_ref, mc_ref, m_ref, mm, ll, oo, al_ref, be_ref, rd, dqt,
-    gblk, keep, rcs, rcr, rxs, rxr, rzs, rzr, zacc,
+    gblk, keep, rcs, rcr, rxs, rxr, rzs, rzr,
     rg_all, pg_all, wsl, dwr, dkeep, dcs, dcr, dxs, dxr, dzs, dzr,
     dq_out, drx_out, dpx_out, dw_out,
     ld_sem, out_sem,
@@ -112,7 +112,7 @@
     loads[2].wait()
 
     def chunk(xx, zz, cc):
-        return pl.ds(al(((xx * NZ + zz) * NC + cc) * PR, PR), PR)
+        return pl.ds(al(((zz * NX + xx) * NC + cc) * PR, PR), PR)
 
     kv[chunk(x, z, c), :] = dot(px[...], w[...]).astype(bf16)
     pl.semaphore_wait(barrier, len(peers))
@@ -132,11 +132,26 @@
         rows = chunk(lax.rem(x - offset(k) + NX, NX), lax.rem(z - j + NZ, NZ), c)
         return remote(kv.at[rows, :], kv.at[rows, :], agc_s.at[k, j], agc_r.at[k, j], core)
 
-    for i in range(3):
+    for i in (1, 0, 2):
         ag_z(i).start()
-    for i in range(3):
+    for i in (2, 0, 1):
         ag_x(0, i).start()
     ag_c(0, 0).start()
+
+    def w_send(o):
+        t2 = lax.rem(tn + o, NT)
+        src = w.at[pl.ds(al(t2 * DT + c * (DT // 2), DT // 2), DT // 2), :]
+        dst = wsl.at[tn, pl.ds(al(c * (DT // 2), DT // 2), DT // 2), :]
+        return remote(src, dst, w_s.at[o - 1], w_r.at[o - 1], dev_t(o))
+
+    def w_core(o):
+        ref = wsl.at[
+            lax.rem(tn - o + NT, NT), pl.ds(al(c * (DT // 2), DT // 2), DT // 2), :
+        ]
+        return remote(ref, ref, wc_s.at[o - 1], wc_r.at[o - 1], core)
+
+    for o in (4, 2, 6):
+        w_send(o).start()
 
     loads[3].wait()
     kv[NP : NP + RL, :] = dot(rx[...], w[...]).astype(bf16)
@@ -151,12 +166,6 @@
         qt[h] = qh.T
         gt[h] = gh.T
     kvt[NX, :, 0:RL] = kv[NP : NP + RL, :].T
-
-    for j in range(1, NZ):
-        ag_z(j - 1).wait_recv()
-        for i in range(3):
-            ag_x(j, i).start()
-        ag_c(0, j).start()
 
     def hc(h):
         return slice(h * RL, (h + 1) * RL)
@@ -209,39 +218,46 @@
 
     pass1(NX, NP, RL, True)
 
+    def along_x(j):
+        ag_z(j - 1).wait_recv()
+        for i in (2, 0, 1):
+            ag_x(j, i).start()
+        ag_c(0, j).start()
+
+    def across(j):
+        for k in (1, 2, 3):
+            ag_x(j, k - 1).wait_recv()
+            ag_c(k, j).start()
+
+    along_x(1)
+    along_x(3)
+    across(0)
+    along_x(2)
+    for o in (3, 5, 1, 7):
+        w_send(o).start()
+
     def block_of(k):
-        return al(lax.rem(x - offset(k) + NX, NX) * BLK, BLK)
+        return al(lax.rem(z - offset(k) + NZ, NZ) * BLK, BLK)
 
     def blocks1(k, _):
-        @pl.when(k < NX - 1)
-        def _():
-            for j in range(NZ):
-                ag_x(j, k).wait_recv()
-                ag_c(k + 1, j).start()
-
-        for j in range(NZ):
-            ag_c(k, j).wait_recv()
+        for i in range(NX):
+            ag_c(i, offset(k)).wait_recv()
         base = block_of(k)
         kvt[k] = kv[pl.ds(base, BLK), :].T
         pass1(k, base, BLK, False)
+
+        @pl.when(k == 0)
+        def _():
+            across(1)
+            across(3)
+
+        @pl.when(k == 1)
+        def _():
+            across(2)
+
         return 0
 
-    lax.fori_loop(0, NX, blocks1, 0)
-
-    def w_send(o):
-        t2 = lax.rem(tn + o, NT)
-        src = w.at[pl.ds(al(t2 * DT + c * (DT // 2), DT // 2), DT // 2), :]
-        dst = wsl.at[tn, pl.ds(al(c * (DT // 2), DT // 2), DT // 2), :]
-        return remote(src, dst, w_s.at[o - 1], w_r.at[o - 1], dev_t(o))
-
-    def w_core(o):
-        ref = wsl.at[
-            lax.rem(tn - o + NT, NT), pl.ds(al(c * (DT // 2), DT // 2), DT // 2), :
-        ]
-        return remote(ref, ref, wc_s.at[o - 1], wc_r.at[o - 1], core)
-
-    for o in range(1, NT):
-        w_send(o).start()
+    lax.fori_loop(0, NZ, blocks1, 0)
 
     for h in range(HEADS):
         rl = 1.0 / ll[h]
@@ -299,29 +315,53 @@
     def rs_c(k):
         return remote(rcs.at[k], rcr.at[k], rc_s.at[k], rc_r.at[k], core)
 
-    def rs_x(k):
-        return remote(rxs.at[k], rxr.at[k], rx_s.at[k], rx_r.at[k], dev_x(NX - offset(NX - 1 - k)))
-
-    def rs_z(i):
-        return remote(rzs.at[i], rzr.at[i], rz_s.at[i], rz_r.at[i], dev_z(i + 1))
+    def rs_x(k, i):
+        return remote(
+            rxs.at[k, i], rxr.at[k, i], rx_s.at[k, i], rx_r.at[k, i], dev_x(offset(i + 1))
+        )
+
+    def rs_z(k):
+        return remote(
+            rzs.at[k], rzr.at[k], rz_s.at[k], rz_r.at[k], dev_z(NZ - offset(NZ - 1 - k))
+        )
+
+    def sum_core(k):
+        rs_c(k).wait_recv()
+        for i in (2, 0, 1):
+            x2 = lax.rem(x + offset(i + 1), NX)
+            rxs[k, i] = (keep[k, x2] + rcr[k, x2].astype(f32)).astype(bf16)
+            rs_x(k, i).start()
+        keep[k, x] = keep[k, x] + rcr[k, x].astype(f32)
+
+    def sum_x(k):
+        tot = keep[k, x]
+        for i in range(NX - 1):
+            rs_x(k, i).wait_recv()
+            tot = tot + rxr[k, i].astype(f32)
+        return tot
+
+    def send_z(k):
+        rzs[k] = sum_x(k).astype(bf16)
+        rs_z(k).start()
 
     def blocks2(k, _):
-        slot = NX - 1 - k
+        slot = NZ - 1 - k
         base = block_of(slot)
         pass2(slot, base, BLK, False, range(0, HEADS // 2))
 
         @pl.when(k > 0)
         def _():
-            rs_c(k - 1).wait_recv()
-            for zz in range(NZ):
-                rxs[k - 1, zz] = (keep[k - 1, zz] + rcr[k - 1, zz].astype(f32)).astype(bf16)
-            rs_x(k - 1).start()
+            sum_core(k - 1)
+
+        @pl.when(k > 1)
+        def _():
+            send_z(k - 2)
 
         pass2(slot, base, BLK, False, range(HEADS // 2, HEADS))
         key_grads(slot, BLK, False)
-        for zz in range(NZ):
-            rcs[k, zz] = gblk[pl.ds(al((zz * NC + oc) * PR, PR), PR), :].astype(bf16)
-            keep[k, zz] = gblk[pl.ds(al((zz * NC + c) * PR, PR), PR), :]
+        for i in range(NX):
+            rcs[k, i] = gblk[pl.ds(al((i * NC + oc) * PR, PR), PR), :].astype(bf16)
+            keep[k, i] = gblk[pl.ds(al((i * NC + c) * PR, PR), PR), :]
         rs_c(k).start()
 
         @pl.when(k == 1)
@@ -332,24 +372,15 @@
 
         return 0
 
-    lax.fori_loop(0, NX, blocks2, 0)
+    lax.fori_loop(0, NZ, blocks2, 0)
+    sum_core(NZ - 1)
 
     for h in range(HEADS):
         dq_out[:, h * HD : (h + 1) * HD] = (dqt[h].T * SCALE).astype(bf16)
     out_dq = pltpu.make_async_copy(dq_out, dq_hbm.at[0], out_sem.at[0])
     out_dq.start()
 
-    rs_c(NX - 1).wait_recv()
-    for k in range(NX - 1):
-        rs_x(k).wait_recv()
-    for zz in range(NZ):
-        tot = keep[NX - 1, zz] + rcr[NX - 1, zz].astype(f32)
-        for k in range(NX - 1):
-            tot = tot + rxr[k, zz].astype(f32)
-        zacc[zz] = tot
-    for i in range(3):
-        rzs[i] = zacc[lax.rem(z + i + 1, NZ)].astype(bf16)
-        rs_z(i).start()
+    send_z(NZ - 2)
 
     for o in range(1, NT):
         w_send(o).wait_recv()
@@ -362,10 +393,9 @@
         rows = slice(i * (DM // NX), (i + 1) * (DM // NX))
         dwr[rows, :] = dot(rxt[rows, :], own_rg)
 
+    tot = sum_x(NZ - 1)
     for i in range(3):
         rs_z(i).wait_recv()
-    tot = zacc[z]
-    for i in range(3):
         tot = tot + rzr[i].astype(f32)
     pg = tot.astype(bf16)
     pg_all[tn] = pg
@@ -464,7 +494,6 @@
         ag_z(i).wait_send()
         for j in range(NZ):
             ag_x(j, i).wait_send()
-        rs_x(i).wait_send()
         rs_z(i).wait_send()
         dw_z(i).wait_send()
     for k in range(NX):
@@ -473,6 +502,7 @@
         rs_c(k).wait_send()
         dw_c(k).wait_send()
         for i in range(NX - 1):
+            rs_x(k, i).wait_send()
             dw_x(k, i).wait_send()
     for o in range(1, NT):
         w_send(o).wait_send()
@@ -484,6 +514,12 @@
         t_fwd(i).wait_send()
     for cp in (out_dq, out_drx, out_dpx, out_dwk, out_dwv):
         cp.wait()
+
+
+def finish(*refs):
+    n = len(refs) // 2
+    for src, dst in zip(refs[:n], refs[n:]):
+        dst[...] = src[...]
 
 
 def local(prompt_x, resp_x, queries, d_attn, w_key, w_value, lengths):
@@ -501,10 +537,10 @@
         v((HEADS, 1, RL), f32), v((HEADS, 1, RL), f32), v((HEADS, HD, RL), f32),
         v((HEADS, 1, RL), f32), v((HEADS, 1, RL), f32), v((HEADS, 1, RL), f32),
         v((HEADS, HD, RL), f32),
-        v((BLK, 2 * HD), f32), v((NX, NZ, PR, 2 * HD), f32),
-        v((NX, NZ, PR, 2 * HD), bf16), v((NX, NZ, PR, 2 * HD), bf16),
-        v((3, NZ, PR, 2 * HD), bf16), v((3, NZ, PR, 2 * HD), bf16),
-        v((3, PR, 2 * HD), bf16), v((3, PR, 2 * HD), bf16), v((NZ, PR, 2 * HD), f32),
+        v((BLK, 2 * HD), f32), v((NZ, NX, PR, 2 * HD), f32),
+        v((NZ, NX, PR, 2 * HD), bf16), v((NZ, NX, PR, 2 * HD), bf16),
+        v((NZ, 3, PR, 2 * HD), bf16), v((NZ, 3, PR, 2 * HD), bf16),
+        v((3, PR, 2 * HD), bf16), v((3, PR, 2 * HD), bf16),
         v((NT, RL, 2 * HD), bf16), v((NT, PR, 2 * HD), bf16), v((NT, DT, 2 * HD), bf16),
         v((DM, 2 * HD), f32), v((NZ, NX, DR, 2 * HD), f32),
         v((NZ, NX, DR, 2 * HD), bf16), v((NZ, NX, DR, 2 * HD), bf16),
@@ -515,19 +551,20 @@
         dma((3,)), dma((3,)), dma((3, NZ)), dma((3, NZ)), dma((NX, NZ)), dma((NX, NZ)),
         dma((NT - 1,)), dma((NT - 1,)), dma((NT - 1,)), dma((NT - 1,)),
         dma((NT - 1,)), dma((NT - 1,)),
-        dma((NX,)), dma((NX,)), dma((3,)), dma((3,)), dma((3,)), dma((3,)),
+        dma((NZ,)), dma((NZ,)), dma((NZ, 3)), dma((NZ, 3)), dma((3,)), dma((3,)),
         dma((NT - 1,)), dma((NT - 1,)),
         dma((NZ,)), dma((NZ,)), dma((NZ, 3)), dma((NZ, 3)), dma((3,)), dma((3,)),
     ]
-    return pl.pallas_call(
+    shapes = (
+        jax.ShapeDtypeStruct((1, RL, HEADS * HD), bf16),
+        jax.ShapeDtypeStruct((1, RL, DT), bf16),
+        jax.ShapeDtypeStruct((PR, DT), bf16),
+        jax.ShapeDtypeStruct((DR, HD), bf16),
+        jax.ShapeDtypeStruct((DR, HD), bf16),
+    )
+    outs = pl.pallas_call(
         kernel,
-        out_shape=(
-            jax.ShapeDtypeStruct((1, RL, HEADS * HD), bf16),
-            jax.ShapeDtypeStruct((1, RL, DT), bf16),
-            jax.ShapeDtypeStruct((PR, DT), bf16),
-            jax.ShapeDtypeStruct((DR, HD), bf16),
-            jax.ShapeDtypeStruct((DR, HD), bf16),
-        ),
+        out_shape=shapes,
         in_specs=[any_] * 6 + [pl.BlockSpec(memory_space=pltpu.SMEM)],
         out_specs=(any_,) * 5,
         scratch_shapes=scratch,
@@ -536,6 +573,14 @@
         ),
         name="kv_backward",
     )(prompt_x, resp_x, queries, d_attn, w_key, w_value, lengths)
+    vmem = pl.BlockSpec(memory_space=pltpu.VMEM)
+    return pl.pallas_call(
+        finish,
+        out_shape=shapes,
+        in_specs=[vmem] * 5,
+        out_specs=(vmem,) * 5,
+        name="finish",
+    )(*outs)
 
 
 def solution(mesh):

time: 100 us -> 81.8 us (0.82)
  Pallas kernels: 93.3 us -> 80.4 us
  local copies, waits for them, and re-layouts: 5.53 us -> 0 us
    pallas_call x1 -> x2, Pallas kernels: 93.3 us -> 80.4 us  [the longest x1 78.3 us: local(): pl.pallas_call(kernel, out_shape=shapes, in_specs=[any_] * 6 + [pl.BlockS...]
    unnamed x11 -> x0, local copies, waits for them, and re-layouts: 5.53 us -> none
where the time goes in v2:
time: 81.8 us; the launch traced here: 81.7 us
  Pallas kernels  80.4 us (98%)
  between operations  1.29 us (2%)
    pallas_call x1, Pallas kernels, local(): pl.pallas_call(kernel, out_shape=shapes, in_specs=[any_] * 6 + [pl.BlockS...  78.3 us
    pallas_call x1, Pallas kernels, local(): pl.pallas_call(finish, out_shape=shapes, in_specs=[vmem] * 5, out_specs=(...  2.16 us

profile of v2, /device:TPU:1, one launch (start us, length us, event | category | flops | bytes accessed | tf_op | source)
XLA Modules:
  0.0 81.7 jit_solution(17983803773446809162)
XLA Ops:
  1.3 78.3 %kv_backward.1 = (bf16[1,256,1024]{2,1,0:T(8,128)(2,1)}, bf16[1,256,640]{2,1,0:T(8,128)(2,1)}, bf16[96,640]{1,0:T(8,128)(2,1)}, bf16[160,128]{1,0:T(8,128)(2,1)}, bf16[160,128]{1,0:T(8,128)(2,1)}) custom-call(bf16[96,5120]{1,0:T(8,128)(2,1)} %px_hbm.1, bf16[1,256,5120]{2,1,0:T(8,128)(2,1)} %rx_hbm.1, bf16[1,256,1024]{2,1,0:T(8,128)(2,1)} %q_hbm.1, ...), custom_call_target="tpu_custom_call" | custom-call | tf_op jit(solution)/shard_map/kv_backward/pallas_call | solution.py:565
  79.6 2.2 %finish.1 = (bf16[1,256,1024]{2,1,0:T(8,128)(2,1)}, bf16[1,256,640]{2,1,0:T(8,128)(2,1)}, bf16[96,640]{1,0:T(8,128)(2,1)}, bf16[160,128]{1,0:T(8,128)(2,1)}, bf16[160,128]{1,0:T(8,128)(2,1)}) custom-call(bf16[1,256,1024]{2,1,0:T(8,128)(2,1)} %get-tuple-element.10.refs_0_, bf16[1,256,640]{2,1,0:T(8,128)(2,1)} %get-tuple-element.11.refs_1_, ...), custom_call_target="tpu_custom_call" | custom-call | tf_op jit(solution)/shard_map/finish/pallas_call | solution.py:577

commit v3 on v2

--- a/solution.py
+++ b/solution.py
@@ -21,6 +21,7 @@
 NP = NZ * BLK
 DM = 5120
 DR = DM // (NX * NZ * NC)
+DX = 128
 DT = DM // NT
 SCALE = HD**-0.5
 SCALE2 = SCALE * math.log2(math.e)
@@ -45,13 +46,14 @@
     kv, kvt, qa, ga, qt, gt,
     e_ref, er_ref, gs_ref, s_ref, mc_ref, m_ref, mm, ll, oo, al_ref, be_ref, rd, dqt,
     gblk, keep, rcs, rcr, rxs, rxr, rzs, rzr,
-    rg_all, pg_all, wsl, dwr, dkeep, dcs, dcr, dxs, dxr, dzs, dzr,
+    rg_all, pg_all, pg2, wsl, dkeep, dcs, dcr, dxs, dxr, dzs, dzr,
+    zfs, zfr, xfs, xfr, xkeep,
     dq_out, drx_out, dpx_out, dw_out,
     ld_sem, out_sem,
     agz_s, agz_r, agx_s, agx_r, agc_s, agc_r,
-    w_s, w_r, wc_s, wc_r, t_s, t_r,
+    w_s, w_r, wc_s, wc_r, pc_s, pc_r, t_s, t_r,
     rc_s, rc_r, rx_s, rx_r, rz_s, rz_r, p_s, p_r,
-    dc_s, dc_r, dx_s, dx_r, dz_s, dz_r,
+    dc_s, dc_r, dx_s, dx_r, dz_s, dz_r, zf_s, zf_r, xf_s, xf_r,
 ):
     sm = lax.axis_index("sample")
     tn = lax.axis_index("tensor")
@@ -90,8 +92,9 @@
     def al(v, n):
         return pl.multiple_of(v, n)
 
+    own_rows = pl.ds(al(c * PR, PR), PR)
     loads = [
-        pltpu.make_async_copy(px_hbm, px, ld_sem.at[0]),
+        pltpu.make_async_copy(px_hbm, px.at[own_rows, :], ld_sem.at[0]),
         pltpu.make_async_copy(wk_hbm, w.at[:, pl.ds(0, HD)], ld_sem.at[1]),
         pltpu.make_async_copy(wv_hbm, w.at[:, pl.ds(HD, HD)], ld_sem.at[2]),
         pltpu.make_async_copy(rx_hbm.at[0], rx, ld_sem.at[3]),
@@ -114,7 +117,7 @@
     def chunk(xx, zz, cc):
         return pl.ds(al(((zz * NX + xx) * NC + cc) * PR, PR), PR)
 
-    kv[chunk(x, z, c), :] = dot(px[...], w[...]).astype(bf16)
+    kv[chunk(x, z, c), :] = dot(px[own_rows, :], w[...]).astype(bf16)
     pl.semaphore_wait(barrier, len(peers))
 
     def ag_z(i):
@@ -152,6 +155,8 @@
 
     for o in (4, 2, 6):
         w_send(o).start()
+
+    px_copy = remote(px.at[own_rows, :], px.at[own_rows, :], pc_s.at[0], pc_r.at[0], core)
 
     loads[3].wait()
     kv[NP : NP + RL, :] = dot(rx[...], w[...]).astype(bf16)
@@ -229,6 +234,7 @@
             ag_x(j, k - 1).wait_recv()
             ag_c(k, j).start()
 
+    rxt[...] = rx[...].T
     along_x(1)
     along_x(3)
     across(0)
@@ -259,14 +265,17 @@
 
     lax.fori_loop(0, NZ, blocks1, 0)
 
+    px_copy.start()
     for h in range(HEADS):
         rl = 1.0 / ll[h]
         rd[h] = jnp.sum(gt[h].astype(f32) * (oo[h] * rl), axis=0, keepdims=True)
         ll[h] = rl
-        dqt[h] = jnp.zeros((HD, RL), f32)
 
     def grads(base, n, h):
         s_ref[h % 2, 0:n, :] = dot(kv[pl.ds(base, n), HD : 2 * HD], gt[h])
+
+    def gslot(slot):
+        return (NZ - slot) // NZ if not isinstance(slot, int) else 0
 
     def gscores(slot, n, h, first):
         fac = jnp.exp2(m_ref[slot, h] - mm[h]) * ll[h]
@@ -277,28 +286,24 @@
             er_ref[:, hc(h)] = pb
         else:
             e_ref[slot, :, hc(h)] = pb
-        gs_ref[0:n, hc(h)] = (p * (s_ref[h % 2, 0:n, :] - rd[h])).astype(bf16)
-
-    def dqs(slot, n, h):
-        dqt[h] += dot(kvt[slot, 0:HD, 0:n], gs_ref[0:n, hc(h)])
-
-    def pass2(slot, base, n, first, heads=range(HEADS)):
-        grads(base, n, heads[0])
-        for h in heads:
-            if h < heads[-1]:
+        gs_ref[gslot(slot), 0:n, hc(h)] = (p * (s_ref[h % 2, 0:n, :] - rd[h])).astype(bf16)
+
+    def pass2(slot, base, n, first):
+        grads(base, n, 0)
+        for h in range(HEADS):
+            if h < HEADS - 1:
                 grads(base, n, h + 1)
             gscores(slot, n, h, first)
-            if h > heads[0]:
-                dqs(slot, n, h - 1)
-        dqs(slot, n, heads[-1])
 
     def key_grads(slot, n, first):
         pb = er_ref[...] if first else e_ref[slot]
-        gblk[0:n, 0:HD] = dot(gs_ref[0:n, :], qa[...]) * SCALE
+        gs = gs_ref[gslot(slot), 0:n, :]
+        gblk[0:n, 0:HD] = dot(gs, qa[...]) * SCALE
         gblk[0:n, HD : 2 * HD] = dot(pb, ga[...])
 
     pass2(NX, NP, RL, True)
     key_grads(NX, RL, True)
+    dqt[...] = dot(kvt[NX, 0:HD, 0:RL], gs_ref[0, 0:RL, :])
     rg_all[tn] = gblk[0:RL, :].astype(bf16)
 
     def t_own(i):
@@ -347,7 +352,7 @@
     def blocks2(k, _):
         slot = NZ - 1 - k
         base = block_of(slot)
-        pass2(slot, base, BLK, False, range(0, HEADS // 2))
+        pass2(slot, base, BLK, False)
 
         @pl.when(k > 0)
         def _():
@@ -357,8 +362,18 @@
         def _():
             send_z(k - 2)
 
-        pass2(slot, base, BLK, False, range(HEADS // 2, HEADS))
+        @pl.when(k == 1)
+        def _():
+            for o in range(1, NT):
+                w_send(o).wait_recv()
+                w_core(o).start()
+
         key_grads(slot, BLK, False)
+
+        @pl.when(k < NZ - 2)
+        def _():
+            dqt[...] += dot(kvt[slot, 0:HD, :], gs_ref[0])
+
         for i in range(NX):
             rcs[k, i] = gblk[pl.ds(al((i * NC + oc) * PR, PR), PR), :].astype(bf16)
             keep[k, i] = gblk[pl.ds(al((i * NC + c) * PR, PR), PR), :]
@@ -373,25 +388,51 @@
         return 0
 
     lax.fori_loop(0, NZ, blocks2, 0)
+
+    def dw_c(g):
+        return remote(dcs.at[g], dcr.at[g], dc_s.at[g], dc_r.at[g], core)
+
+    def dw_x(g, i):
+        return remote(
+            dxs.at[g, i], dxr.at[g, i], dx_s.at[g, i], dx_r.at[g, i], dev_x(offset(3 - i))
+        )
+
+    def dw_z(g):
+        return remote(dzs.at[g], dzr.at[g], dz_s.at[g], dz_r.at[g], dev_z(offset(3 - g)))
+
+    def zf(g):
+        return remote(zfs.at[g], zfr.at[g], zf_s.at[g], zf_r.at[g], dev_z(offset(3 - g)))
+
+    def xf(i):
+        return remote(xfs.at[i], xfr.at[i], xf_s.at[i], xf_r.at[i], dev_x(offset(3 - i)))
+
+    def dw_rows(g, i, cc):
+        zz = lax.rem(z + offset(3 - g), NZ)
+        xx = lax.rem(x + offset(3 - i), NX)
+        return pl.ds(al(((xx * NZ + zz) * NC + cc) * DR, DR), DR)
+
+    own_rg = rg_all[tn]
+
+    def dw_resp(g, _):
+        for i in range(NX):
+            dcs[g, i] = dot(rxt[dw_rows(g, i, oc), :], own_rg).astype(bf16)
+            dkeep[g, i] = dot(rxt[dw_rows(g, i, c), :], own_rg)
+        dw_c(g).start()
+        return 0
+
+    lax.fori_loop(0, NZ, dw_resp, 0)
     sum_core(NZ - 1)
-
-    for h in range(HEADS):
-        dq_out[:, h * HD : (h + 1) * HD] = (dqt[h].T * SCALE).astype(bf16)
-    out_dq = pltpu.make_async_copy(dq_out, dq_hbm.at[0], out_sem.at[0])
-    out_dq.start()
-
     send_z(NZ - 2)
-
-    for o in range(1, NT):
-        w_send(o).wait_recv()
-        w_core(o).start()
-    wsl[tn] = w[pl.ds(al(tn * DT, DT), DT), :]
+    px_copy.wait_recv()
     pxt[...] = px[...].T
-    rxt[...] = rx[...].T
-    own_rg = rg_all[tn]
-    for i in range(NX):
-        rows = slice(i * (DM // NX), (i + 1) * (DM // NX))
-        dwr[rows, :] = dot(rxt[rows, :], own_rg)
+
+    def dw_both(g, _):
+        dw_c(g).wait_recv()
+        for i in range(NX):
+            dkeep[g, i] = dkeep[g, i] + dcr[g, i].astype(f32)
+        return 0
+
+    lax.fori_loop(0, NZ, dw_both, 0)
 
     tot = sum_x(NZ - 1)
     for i in range(3):
@@ -403,48 +444,57 @@
     def p_send(o):
         return remote(pg_all.at[tn], pg_all.at[tn], p_s.at[o - 1], p_r.at[o - 1], dev_t(o))
 
-    def dw_c(g):
-        return remote(dcs.at[g], dcr.at[g], dc_s.at[g], dc_r.at[g], core)
-
-    def dw_x(g, i):
-        return remote(
-            dxs.at[g, i], dxr.at[g, i], dx_s.at[g, i], dx_r.at[g, i], dev_x(offset(3 - i))
-        )
-
-    def dw_z(g):
-        return remote(dzs.at[g], dzr.at[g], dz_s.at[g], dz_r.at[g], dev_z(offset(3 - g)))
-
-    def dw_group(g, _):
-        zz = lax.rem(z + offset(3 - g), NZ)
-        for i in range(NX):
-            xx = lax.rem(x + offset(3 - i), NX)
-            first = (xx * NZ + zz) * NC
-            theirs = pl.ds(al((first + oc) * DR, DR), DR)
-            mine = pl.ds(al((first + c) * DR, DR), DR)
-            dcs[g, i] = (dwr[theirs, :] + dot(pxt[theirs, :], pg)).astype(bf16)
-            dkeep[g, i] = dwr[mine, :] + dot(pxt[mine, :], pg)
-        dw_c(g).start()
-        return 0
-
-    lax.fori_loop(0, NZ, dw_group, 0)
+    pg2[own_rows, :] = pg
+    pg_copy = remote(pg2.at[own_rows, :], pg2.at[own_rows, :], pc_s.at[1], pc_r.at[1], core)
+    pg_copy.start()
     for o in range(1, NT):
         p_send(o).start()
+    pg_copy.wait_recv()
+    pg_both = pg2[...]
 
     def dw_sum(g, _):
-        dw_c(g).wait_recv()
-        for i in range(NX - 1):
-            dxs[g, i] = (dkeep[g, i] + dcr[g, i].astype(f32)).astype(bf16)
-            dw_x(g, i).start()
-        dkeep[g, NX - 1] = dkeep[g, NX - 1] + dcr[g, NX - 1].astype(f32)
+        for i in range(NX):
+            tot = dkeep[g, i] + dot(pxt[dw_rows(g, i, c), :], pg_both)
+            dkeep[g, i] = tot
+            if i < NX - 1:
+                dxs[g, i] = tot[0:DX].astype(bf16)
+                dw_x(g, i).start()
+
+        @pl.when(g < NZ - 1)
+        def _():
+            for i in range(NX):
+                zfs[g, i] = dkeep[g, i, DX:DR, :].astype(bf16)
+            zf(g).start()
+
         return 0
 
     lax.fori_loop(0, NZ, dw_sum, 0)
+
+    for k in range(2):
+        dqt[...] += dot(kvt[k, 0:HD, :], gs_ref[1 - k])
+    for h in range(HEADS):
+        dq_out[:, h * HD : (h + 1) * HD] = (dqt[:, hc(h)].T * SCALE).astype(bf16)
+    out_dq = pltpu.make_async_copy(dq_out, dq_hbm.at[0], out_sem.at[0])
+    out_dq.start()
+
+    for g in range(NZ - 1):
+        zf(g).wait_recv()
+    for i in range(NX):
+        tot = dkeep[NZ - 1, i, DX:DR, :]
+        for g in range(NZ - 1):
+            tot = tot + zfr[g, i].astype(f32)
+        if i < NX - 1:
+            xfs[i] = tot.astype(bf16)
+            xf(i).start()
+        else:
+            xkeep[...] = tot
 
     for i in range(1, 4):
         t_own(i).wait_recv()
         t_fwd(i).wait_recv()
     for o in range(1, NT):
         w_core(o).wait_recv()
+    wsl[tn] = w[pl.ds(al(tn * DT, DT), DT), :]
     acc = dot_t(rg_all[0], wsl[0])
     for t2 in range(1, NT):
         acc = acc + dot_t(rg_all[t2], wsl[t2])
@@ -455,10 +505,10 @@
     def dw_last(g, _):
         for i in range(NX - 1):
             dw_x(g, i).wait_recv()
-        tot = dkeep[g, NX - 1]
+        tot = dkeep[g, NX - 1, 0:DX, :]
         for i in range(NX - 1):
             tot = tot + dxr[g, i].astype(f32)
-        dkeep[g, NX - 1] = tot
+        dkeep[g, NX - 1, 0:DX, :] = tot
 
         @pl.when(g < NZ - 1)
         def _():
@@ -480,11 +530,17 @@
 
     for g in range(NZ - 1):
         dw_z(g).wait_recv()
-    tot = dkeep[NZ - 1, NX - 1]
+    tot = dkeep[NZ - 1, NX - 1, 0:DX, :]
     for g in range(NZ - 1):
         tot = tot + dzr[g].astype(f32)
-    dw_out[0] = tot[:, 0:HD].astype(bf16)
-    dw_out[1] = tot[:, HD : 2 * HD].astype(bf16)
+    dw_out[0, 0:DX, :] = tot[:, 0:HD].astype(bf16)
+    dw_out[1, 0:DX, :] = tot[:, HD : 2 * HD].astype(bf16)
+    tot = xkeep[...]
+    for i in range(NX - 1):
+        xf(i).wait_recv()
+        tot = tot + xfr[i].astype(f32)
+    dw_out[0, DX:DR, :] = tot[:, 0:HD].astype(bf16)
+    dw_out[1, DX:DR, :] = tot[:, HD : 2 * HD].astype(bf16)
     out_dwk = pltpu.make_async_copy(dw_out.at[0], dwk_hbm, out_sem.at[3])
     out_dwv = pltpu.make_async_copy(dw_out.at[1], dwv_hbm, out_sem.at[4])
     out_dwk.start()
@@ -496,6 +552,8 @@
             ag_x(j, i).wait_send()
         rs_z(i).wait_send()
         dw_z(i).wait_send()
+        zf(i).wait_send()
+        xf(i).wait_send()
     for k in range(NX):
         for j in range(NZ):
             ag_c(k, j).wait_send()
@@ -508,6 +566,8 @@
         w_send(o).wait_send()
         w_core(o).wait_send()
         p_send(o).wait_send()
+    px_copy.wait_send()
+    pg_copy.wait_send()
     for i in range(4):
         t_own(i).wait_send()
     for i in range(1, 4):
@@ -527,33 +587,38 @@
     v = pltpu.VMEM
     dma = pltpu.SemaphoreType.DMA
     scratch = [
-        v((PR, DM), bf16), v((RL, DM), bf16), v((RL, HEADS * HD), bf16), v((RL, HEADS * HD), bf16),
-        v((DM, 2 * HD), bf16), v((DM, RL), bf16), v((DM, PR), bf16),
+        v((NC * PR, DM), bf16), v((RL, DM), bf16), v((RL, HEADS * HD), bf16), v((RL, HEADS * HD), bf16),
+        v((DM, 2 * HD), bf16), v((DM, RL), bf16), v((DM, NC * PR), bf16),
         v((NP + RL, 2 * HD), bf16), v((NX + 1, 2 * HD, BLK), bf16),
         v((HEADS * RL, HD), bf16), v((HEADS * RL, HD), bf16),
         v((HEADS, HD, RL), bf16), v((HEADS, HD, RL), bf16),
-        v((NX, BLK, HEADS * RL), bf16), v((RL, HEADS * RL), bf16), v((BLK, HEADS * RL), bf16),
+        v((NZ, BLK, HEADS * RL), bf16), v((RL, HEADS * RL), bf16),
+        v((2, BLK, HEADS * RL), bf16),
         v((2, BLK, RL), f32), v((2, 1, RL), f32), v((NX + 1, HEADS, 1, RL), f32),
         v((HEADS, 1, RL), f32), v((HEADS, 1, RL), f32), v((HEADS, HD, RL), f32),
         v((HEADS, 1, RL), f32), v((HEADS, 1, RL), f32), v((HEADS, 1, RL), f32),
-        v((HEADS, HD, RL), f32),
+        v((HD, HEADS * RL), f32),
         v((BLK, 2 * HD), f32), v((NZ, NX, PR, 2 * HD), f32),
         v((NZ, NX, PR, 2 * HD), bf16), v((NZ, NX, PR, 2 * HD), bf16),
         v((NZ, 3, PR, 2 * HD), bf16), v((NZ, 3, PR, 2 * HD), bf16),
         v((3, PR, 2 * HD), bf16), v((3, PR, 2 * HD), bf16),
-        v((NT, RL, 2 * HD), bf16), v((NT, PR, 2 * HD), bf16), v((NT, DT, 2 * HD), bf16),
-        v((DM, 2 * HD), f32), v((NZ, NX, DR, 2 * HD), f32),
+        v((NT, RL, 2 * HD), bf16), v((NT, PR, 2 * HD), bf16), v((NC * PR, 2 * HD), bf16),
+        v((NT, DT, 2 * HD), bf16), v((NZ, NX, DR, 2 * HD), f32),
         v((NZ, NX, DR, 2 * HD), bf16), v((NZ, NX, DR, 2 * HD), bf16),
-        v((NZ, NX - 1, DR, 2 * HD), bf16), v((NZ, NX - 1, DR, 2 * HD), bf16),
-        v((NZ - 1, DR, 2 * HD), bf16), v((NZ - 1, DR, 2 * HD), bf16),
+        v((NZ, NX - 1, DX, 2 * HD), bf16), v((NZ, NX - 1, DX, 2 * HD), bf16),
+        v((NZ - 1, DX, 2 * HD), bf16), v((NZ - 1, DX, 2 * HD), bf16),
+        v((NZ - 1, NX, DR - DX, 2 * HD), bf16), v((NZ - 1, NX, DR - DX, 2 * HD), bf16),
+        v((NX - 1, DR - DX, 2 * HD), bf16), v((NX - 1, DR - DX, 2 * HD), bf16),
+        v((DR - DX, 2 * HD), f32),
         v((RL, HEADS * HD), bf16), v((RL, DT), bf16), v((PR, DT), bf16), v((2, DR, HD), bf16),
         dma((6,)), dma((5,)),
         dma((3,)), dma((3,)), dma((3, NZ)), dma((3, NZ)), dma((NX, NZ)), dma((NX, NZ)),
-        dma((NT - 1,)), dma((NT - 1,)), dma((NT - 1,)), dma((NT - 1,)),
+        dma((NT - 1,)), dma((NT - 1,)), dma((NT - 1,)), dma((NT - 1,)), dma((2,)), dma((2,)),
         dma((NT - 1,)), dma((NT - 1,)),
         dma((NZ,)), dma((NZ,)), dma((NZ, 3)), dma((NZ, 3)), dma((3,)), dma((3,)),
         dma((NT - 1,)), dma((NT - 1,)),
         dma((NZ,)), dma((NZ,)), dma((NZ, 3)), dma((NZ, 3)), dma((3,)), dma((3,)),
+        dma((3,)), dma((3,)), dma((3,)), dma((3,)),
     ]
     shapes = (
         jax.ShapeDtypeStruct((1, RL, HEADS * HD), bf16),

time: 81.8 us -> 80.9 us (0.989)
  Pallas kernels: 80.4 us -> 79.5 us
    pallas_call x1, Pallas kernels: 78.3 us -> 77.3 us  [local(): pl.pallas_call(kernel, out_shape=shapes, in_specs=[any_] * 6 + [pl.BlockS...]
where the time goes in v3:
time: 80.9 us; the launch traced here: 80.8 us
  Pallas kernels  79.5 us (98%)
  between operations  1.29 us (2%)
    pallas_call x1, Pallas kernels, local(): pl.pallas_call(kernel, out_shape=shapes, in_specs=[any_] * 6 + [pl.BlockS...  77.3 us
    pallas_call x1, Pallas kernels, local(): pl.pallas_call(finish, out_shape=shapes, in_specs=[vmem] * 5, out_specs=(...  2.16 us

profile of v3, /device:TPU:1, one launch (start us, length us, event | category | flops | bytes accessed | tf_op | source)
XLA Modules:
  0.0 80.8 jit_solution(15703508624676923444)
XLA Ops:
  1.3 77.3 %kv_backward.1 = (bf16[1,256,1024]{2,1,0:T(8,128)(2,1)}, bf16[1,256,640]{2,1,0:T(8,128)(2,1)}, bf16[96,640]{1,0:T(8,128)(2,1)}, bf16[160,128]{1,0:T(8,128)(2,1)}, bf16[160,128]{1,0:T(8,128)(2,1)}) custom-call(bf16[96,5120]{1,0:T(8,128)(2,1)} %px_hbm.1, bf16[1,256,5120]{2,1,0:T(8,128)(2,1)} %rx_hbm.1, bf16[1,256,1024]{2,1,0:T(8,128)(2,1)} %q_hbm.1, ...), custom_call_target="tpu_custom_call" | custom-call | tf_op jit(solution)/shard_map/kv_backward/pallas_call | solution.py:630
  78.6 2.2 %finish.1 = (bf16[1,256,1024]{2,1,0:T(8,128)(2,1)}, bf16[1,256,640]{2,1,0:T(8,128)(2,1)}, bf16[96,640]{1,0:T(8,128)(2,1)}, bf16[160,128]{1,0:T(8,128)(2,1)}, bf16[160,128]{1,0:T(8,128)(2,1)}) custom-call(bf16[1,256,1024]{2,1,0:T(8,128)(2,1)} %get-tuple-element.10.refs_0_, bf16[1,256,640]{2,1,0:T(8,128)(2,1)} %get-tuple-element.11.refs_1_, ...), custom_call_target="tpu_custom_call" | custom-call | tf_op jit(solution)/shard_map/finish/pallas_call | solution.py:642
